TPU v7x, 32 devices: a whole 2x2x4 slice. The times are simulated.
32 devices in a mesh: section: 4 (over z), dp: 2 (over core), tensor: 4 (over y, x).
Axes of the slice: x: 2, y: 2, z: 4, core: 2. Of those that a mesh axis runs over, the one named last changes fastest.
Arguments:
- patches: bfloat16 [6144, 1280], P(('section', 'dp')), may hold values from -6 to 6
- window_ids: int32 [6144], P(('section', 'dp')), may hold values from 0 to 152, never falling along the last dimension, each value on 1 to 64 neighbouring positions
- norm_gain: float32 [1280], replicated, may hold values from 0.25 to 1.75
- w_qkv: bfloat16 [1280, 3, 1280], P(('section', 'dp'), None, 'tensor'), may hold values from -0.15625 to 0.15625
- qkv_bias: float32 [3, 1280], P(None, 'tensor'), may hold values from -10 to 10
- w_out: bfloat16 [1280, 1280], P(('section', 'dp'), 'tensor'), may hold values from -0.15625 to 0.15625
Outputs:
- mixed: bfloat16 [6144, 1280], P(('section', 'dp'))
Inputs may be any that keep to these rules, and one draw needn't show every extreme that they name: window_ids never fall along the packed order; each window holds 1 to 64 consecutive patches, and some window holds exactly 64.
All inputs are finite; a program needn't handle non-finite values.
Results may differ from a plain program's by a relative error of at most 0.012.
Values may be sent and summed in bfloat16 or wider, within the bound.
A program may use at most 64 MiB of HBM per device.

v0:
```python
import jax
import jax.numpy as jnp
from jax import lax
from jax.sharding import PartitionSpec as P

HEAD = 80
WIN = 64


def with_halo(cells, sides, width):
    for axis, dim in sides:
        count = lax.axis_size(axis)
        ends = count - 1
        head = lax.slice_in_dim(cells, 0, width, axis=dim)
        tail = lax.slice_in_dim(cells, cells.shape[dim] - width, cells.shape[dim], axis=dim)
        cells = jnp.concatenate(
            [
                lax.ppermute(tail, axis, [(i, (i + 1) % count) for i in range(ends)]),
                cells,
                lax.ppermute(head, axis, [((i + 1) % count, i) for i in range(ends)]),
            ],
            axis=dim,
        )
    return cells


def local(patches, window_ids, norm_gain, w_qkv, qkv_bias, w_out):
    rows = patches.shape[0]
    local_cols = w_qkv.shape[2]
    local_heads = local_cols // HEAD
    values_f = patches.astype(jnp.float32)
    scale_row = lax.rsqrt(jnp.mean(values_f * values_f, axis=-1, keepdims=True) + 1e-06)
    normed = (values_f * scale_row * norm_gain).astype(jnp.bfloat16)
    piece = lax.all_gather(w_qkv, ("section", "dp"), axis=0, tiled=True)
    count = piece.shape[0]
    proj = jnp.dot(normed, piece.reshape(count, 3 * local_cols), preferred_element_type=jnp.float32)
    proj = (proj + qkv_bias.reshape(3 * local_cols)).astype(jnp.bfloat16)
    keyvals = with_halo(proj[:, local_cols:], ((("section", "dp"), 0),), WIN)
    marks = with_halo(window_ids + 1, ((("section", "dp"), 0),), WIN)
    block_rows = 128
    blocks = rows // block_rows
    key_span = block_rows + 2 * WIN
    queries = proj[:, :local_cols].reshape(blocks, block_rows, local_heads, HEAD)
    kv_blocks = jnp.stack(
        [keyvals[i * block_rows : i * block_rows + key_span] for i in range(blocks)]
    )
    mark_blocks = jnp.stack(
        [marks[i * block_rows : i * block_rows + key_span] for i in range(blocks)]
    )
    keys = kv_blocks[:, :, :local_cols].reshape(blocks, key_span, local_heads, HEAD)
    vals = kv_blocks[:, :, local_cols:].reshape(blocks, key_span, local_heads, HEAD)
    mark_q = marks[WIN : WIN + rows].reshape(blocks, block_rows)
    allowed = mark_q[:, :, None] == mark_blocks[:, None, :]
    factor = 1.0 / HEAD**0.5
    scores = (
        jnp.einsum("bqhd,bkhd->bhqk", queries, keys, preferred_element_type=jnp.float32) * factor
    )
    scores = jnp.where(allowed[:, None], scores, jnp.float32(-1e30))
    top = jnp.max(scores, axis=-1, keepdims=True)
    expo = jnp.where(allowed[:, None], jnp.exp(scores - top), jnp.float32(0.0))
    probs = (expo / jnp.sum(expo, axis=-1, keepdims=True)).astype(jnp.bfloat16)
    attn = jnp.einsum("bhqk,bkhd->bqhd", probs, vals, preferred_element_type=jnp.float32)
    attn = attn.reshape(rows, local_cols).astype(jnp.bfloat16)
    partial_out = lax.dot_general(
        attn,
        lax.all_gather(w_out, ("section", "dp"), axis=0, tiled=True),
        (((1,), (1,)), ((), ())),
        preferred_element_type=jnp.float32,
    )
    summed = lax.psum(partial_out.astype(jnp.bfloat16), "tensor").astype(jnp.float32)
    return (values_f + summed).astype(jnp.bfloat16)


def solution(mesh):
    placed = (
        P(("section", "dp"), None),
        P(("section", "dp")),
        P(),
        P(("section", "dp"), None, "tensor"),
        P(None, "tensor"),
        P(("section", "dp"), "tensor"),
    )
    return jax.shard_map(
        local, mesh=mesh, in_specs=placed, out_specs=P(("section", "dp"), None), check_vma=False
    )
```

profile of v0, /device:TPU:0, one launch (start us, length us, event | category | flops | bytes accessed | tf_op | source)
XLA Modules:
  0.0 164.3 jit_solution(382785309299708029)
XLA Ops:
  6.5 0.7 all-gather.2.cloned.1.call-update
  7.3 0.0 all-reduce.2.cloned.1.call-start
  7.3 0.7 fusion.32
  8.0 0.1 fusion.35
  8.1 2.3 %collective-permute-start.2 = (s32[64]{0:T(128)S(1)}, s32[64]{0:T(128)S(1)}, u32[]{:S(2)}, u32[]{:S(2)}) collective-permute-start(s32[64]{0:T(128)S(1)} %get-tuple-element.14), channel_id=1, source_target_pairs={{0,4},{4,8},{8,12},{12,16},{16,20},{20,24},{24,28},{1,5},{5,9},{9,... | collective-permute-start | bytes 776 | tf_op jit(solution)/shard_map/ppermute | solution.py:18
  10.4 1.3 collective-permute-start.3
  11.7 0.1 fusion.36
  11.8 2.0 %fusion.1 = f32[768]{0:T(1024)S(1)} fusion(bf16[768,1280]{1,0:T(8,128)(2,1)} %param.6), kind=kLoop, calls=%fused_computation.4 | loop fusion | flops 2948352 | bytes 1969152 | tf_op jit(solution)/shard_map/reduce_sum | solution.py:32
  13.8 27.3 %all_gather.7 = bf16[1280,320]{1,0:T(8,128)(2,1)} all-gather(bf16[160,320]{1,0:T(8,128)(2,1)} %param.11), channel_id=1, replica_groups=mesh['section'=4,'dp'=2,'tensor'=4] {'section','dp'}, dimensions={0}, use_global_device_ids=true | all-gather | bytes 921600 | tf_op jit(solution)/shard_map/all_gather | solution.py:66
  41.1 0.1 add.34
  41.2 0.0 collective-permute-done.2
  41.2 0.0 collective-permute-done.3
  41.2 0.1 pad_add_fusion.1
  41.3 0.1 slice.87
  41.4 0.0 copy-start
  41.4 0.0 copy-start.6
  41.4 14.1 %all-gather.2.cloned.1.call-done = bf16[1280,3,320]{2,0,1:T(8,128)(2,1)} async-done(((bf16[160,3,320]{2,0,1:T(8,128)(2,1)}), bf16[1280,3,320]{2,0,1:T(8,128)(2,1)}) %all-gather.2.cloned.1.call-update) | async-done | bytes 2457616 | tf_op jit(solution)/shard_map/all_gather | solution.py:34
  55.5 5.3 %copy.11 = bf16[1280,3,320]{0,2,1:T(8,128)(2,1)} copy(bf16[1280,3,320]{2,0,1:T(8,128)(2,1)} %all-gather.2.cloned.1.call-done) | data formatting | bytes 4915200 | tf_op jit(solution)/shard_map/all_gather | solution.py:34
  60.8 0.0 copy-done.6
  60.8 3.9 %add_convert_fusion = bf16[768,960]{0,1:T(8,128)(2,1)S(1)} fusion(bf16[1280,960]{0,1:T(8,128)(2,1)} %bitcast.51, bf16[768,1280]{1,0:T(8,128)(2,1)S(1)} %copy-done, f32[1280]{0:T(1024)S(1)} %copy-done.6, f32[768]{0:T(1024)S(1)} %add_rsqrt_fusion, f32[960]{0:T(1024)S(1)} %add.34), kind=kOutput, calls=%fused_computation.12 | convolution fusion | flops 1892843520 | bytes 5910272 | tf_op jit(solution)/shard_map/dot_general | solution.py:36
  64.7 0.0 copy-start.1
  64.7 0.9 fusion.34
  65.6 2.8 %collective-permute-start = (bf16[64,640]{0,1:T(8,128)(2,1)}, bf16[64,640]{0,1:T(8,128)(2,1)}, u32[]{:S(2)}, u32[]{:S(2)}) collective-permute-start(bf16[64,640]{0,1:T(8,128)(2,1)} %get-tuple-element.8), channel_id=1, source_target_pairs={{0,4},{4,8},{8,12},{12,16},{16,20},{20,24},{24,28},{1,5},{5,9},{9,... | collective-permute-start | bytes 245768 | tf_op jit(solution)/shard_map/ppermute | solution.py:18
  68.4 0.9 broadcast_compare_fusion
  69.3 0.1 slice.91
  69.4 1.3 collective-permute-start.1
  70.7 1.4 reshape.31
  72.1 0.0 collective-permute-done
  72.1 1.1 fusion.29
  73.2 1.2 fusion.27
  74.4 1.2 fusion.26
  75.6 1.2 fusion.25
  76.8 1.2 fusion.24
  78.0 0.0 copy-start.2
  78.0 0.0 collective-permute-done.1
  78.0 1.2 fusion.23
  79.2 0.1 fusion.33
  79.3 0.6 fusion.20
  80.0 0.3 copy-done.4
  80.3 1.8 %fusion.37 = (f32[6,4,128]{2,1,0:T(4,128)S(1)}, f32[6,4,128,256]{3,2,1,0:T(8,128)S(1)}) fusion(f32[6,4,128,256]{3,2,1,0:T(8,128)S(1)} %fusion.20, pred[6,128,256]{2,1,0:T(8,128)(4,1)S(1)} %copy-done.4), kind=kOutput, calls=%fused_computation.53 | output fusion | flops 5505279 | bytes 6500352 | tf_op jit(solution)/shard_map/sub | solution.py:60
  82.0 0.0 copy-start.3
  82.0 0.8 fusion.17
  82.8 0.3 copy.13
  83.1 0.1 copy-done.3
  83.2 2.5 %convolution_convert_fusion = bf16[768,1280]{1,0:T(8,128)(2,1)} fusion(bf16[1280,320]{1,0:T(8,128)(2,1)S(1)} %copy-done.3, bf16[40,8,6,128]{3,2,1,0:T(8,128)(2,1)S(1)} %bitcast.53), kind=kOutput, calls=%fused_computation.8 | convolution fusion | flops 630128640 | bytes 3276800 | tf_op jit(solution)/shard_map/dot_general | solution.py:64
  85.7 0.0 all-reduce.2.cloned.1.call-update
  85.7 68.4 %all-reduce.2.cloned.1.call-done = bf16[768,1280]{1,0:T(8,128)(2,1)} async-done(((bf16[768,1280]{1,0:T(8,128)(2,1)}), bf16[768,1280]{1,0:T(8,128)(2,1)}) %all-reduce.2.cloned.1.call-update) | async-done | bytes 1966096 | tf_op jit(solution)/shard_map/psum | solution.py:70
  154.2 3.3 %fusion.4 = bf16[768,1280]{1,0:T(8,128)(2,1)} fusion(bf16[768,1280]{1,0:T(8,128)(2,1)S(1)} %copy-done, bf16[768,1280]{1,0:T(8,128)(2,1)} %all-reduce.2.cloned.1.call-done), kind=kLoop, calls=%fused_computation.7 | loop fusion | flops 3932160 | bytes 5898240 | tf_op jit(solution)/shard_map/convert_element_type | solution.py:71
  (11 shorter events, 0.1 us)
Async XLA Ops:
  6.5 34.6 %copy-start.5 = (f32[3,320]{1,0:T(4,128)S(1)}, f32[3,320]{1,0:T(4,128)}, u32[]{:S(2)}) copy-start(f32[3,320]{1,0:T(4,128)} %param.10) | copy-start | bytes 11524
  6.5 48.9 %all-gather.2.cloned.1.call-start = ((), (), s32[]{:S(2)}) async-start(), calls=%async_computation | async-start | bytes 3317760 | tf_op jit(solution)/shard_map/all_gather | solution.py:34
  7.3 146.9 %all-reduce.2.cloned.1.call-start = ((), (), s32[]{:S(2)}) async-start(), calls=%async_computation.1 | async-start | bytes 3932160 | tf_op jit(solution)/shard_map/psum | solution.py:70
  8.1 33.1 %collective-permute-start.2 = (s32[64]{0:T(128)S(1)}, s32[64]{0:T(128)S(1)}, u32[]{:S(2)}, u32[]{:S(2)}) collective-permute-start(s32[64]{0:T(128)S(1)} %get-tuple-element.14), channel_id=1, source_target_pairs={{0,4},{4,8},{8,12},{12,16},{16,20},{20,24},{24,28},{1,5},{5,9},{9,... | collective-permute-start | bytes 776 | tf_op jit(solution)/shard_map/ppermute | solution.py:18
  10.4 30.8 %collective-permute-start.3 = (s32[64]{0:T(128)S(1)}, s32[64]{0:T(128)S(1)}, u32[]{:S(2)}, u32[]{:S(2)}) collective-permute-start(s32[64]{0:T(128)S(1)} %get-tuple-element.13), channel_id=1, source_target_pairs={{4,0},{8,4},{12,8},{16,12},{20,16},{24,20},{28,24},{5,1},{9,5},{13... | collective-permute-start | bytes 776 | tf_op jit(solution)/shard_map/ppermute | solution.py:20
  41.4 19.4 %copy-start = (bf16[768,1280]{1,0:T(8,128)(2,1)S(1)}, bf16[768,1280]{1,0:T(8,128)(2,1)}, u32[]{:S(2)}) copy-start(bf16[768,1280]{1,0:T(8,128)(2,1)} %param.6) | copy-start | bytes 5898244
  41.4 19.4 %copy-start.6 = (f32[1280]{0:T(1024)S(1)}, f32[1280]{0:T(1024)}, u32[]{:S(2)}) copy-start(f32[1280]{0:T(1024)} %param.8) | copy-start | bytes 15364
  64.7 4.7 %copy-start.1 = (bf16[768,960]{0,1:T(8,128)(2,1)}, bf16[768,960]{0,1:T(8,128)(2,1)S(1)}, u32[]{:S(2)}) copy-start(bf16[768,960]{0,1:T(8,128)(2,1)S(1)} %add_convert_fusion) | copy-start | bytes 4423684
  65.6 6.5 %collective-permute-start = (bf16[64,640]{0,1:T(8,128)(2,1)}, bf16[64,640]{0,1:T(8,128)(2,1)}, u32[]{:S(2)}, u32[]{:S(2)}) collective-permute-start(bf16[64,640]{0,1:T(8,128)(2,1)} %get-tuple-element.8), channel_id=1, source_target_pairs={{0,4},{4,8},{8,12},{12,16},{16,20},{20,24},{24,28},{1,5},{5,9},{9,... | collective-permute-start | bytes 245768 | tf_op jit(solution)/shard_map/ppermute | solution.py:18
  69.4 8.6 %collective-permute-start.1 = (bf16[64,640]{0,1:T(8,128)(2,1)}, bf16[64,640]{0,1:T(8,128)(2,1)}, u32[]{:S(2)}, u32[]{:S(2)}) collective-permute-start(bf16[64,640]{0,1:T(8,128)(2,1)} %get-tuple-element.7), channel_id=1, source_target_pairs={{4,0},{8,4},{12,8},{16,12},{20,16},{24,20},{28,24},{5,1},{9,5},{13... | collective-permute-start | bytes 245768 | tf_op jit(solution)/shard_map/ppermute | solution.py:20
  78.0 1.4 copy-start.2
  79.3 0.9 copy-start.4
  82.0 1.2 copy-start.3
Sparse Core Ops, SparseCore 0:
  9.0 46.4 all-gather.1
  85.9 68.2 all-reduce.1
where the time goes:
time: 165 us; the launch traced here: 164 us
  waiting for transfers between devices  83.2 us (50%)
  blocking collectives  27.3 us (17%)
  local copies, waits for them, and re-layouts  13.7 us (8%)
  between operations  13.6 us (8%)
  other arithmetic  10.9 us (7%)
  starting transfers between devices  7.79 us (5%)
  matrix products  7.75 us (5%)
    psum x1, waiting for transfers between devices, local(): lax.psum(partial_out.astype(jnp.bfloat16), 'tensor').astype(jnp.float32)  68.4 us
    all_gather x1, blocking collectives, local(): lax.all_gather(w_out, ('section', 'dp'), axis=0, tiled=True)  27.3 us
    all_gather x1, waiting for transfers between devices, local(): piece = lax.all_gather(w_qkv, ('section', 'dp'), axis=0, tiled=True)  14.1 us
    all_gather x1, local copies, waits for them, and re-layouts, local(): piece = lax.all_gather(w_qkv, ('section', 'dp'), axis=0, tiled=True)  5.29 us
    unnamed x18, local copies, waits for them, and re-layouts  5.19 us
    ppermute x2, starting transfers between devices, with_halo(): lax.ppermute(tail, axis, [(i, (i + 1) % count) for i in range(ends)])  5.16 us
    dot_general x1, matrix products, local(): jnp.dot(normed, piece.reshape(count, 3 * local_cols), preferred_element_t...  3.88 us
  transfers between devices with their start and end apart: 6, of which 2 were waited for; matrix products, arithmetic and copies ran while one was open for 7% of the time, Pallas kernels for 0%

commit v1 on v0

--- a/solution.py
+++ b/solution.py
@@ -67,7 +67,9 @@
         (((1,), (1,)), ((), ())),
         preferred_element_type=jnp.float32,
     )
-    summed = lax.psum(partial_out.astype(jnp.bfloat16), "tensor").astype(jnp.float32)
+    summed = jnp.sum(lax.all_gather(partial_out.astype(jnp.bfloat16), "tensor"), axis=0).astype(
+        jnp.float32
+    )
     return (values_f + summed).astype(jnp.bfloat16)
 
 

time: 165 us -> 182 us (1.10)
  waiting for transfers between devices: 83.2 us -> 100 us
  other arithmetic: 10.9 us -> 15.9 us
  local copies, waits for them, and re-layouts: 13.7 us -> 10.2 us
  blocking collectives: 27.3 us -> 25.4 us
    all_gather x0 -> x1, waiting for transfers between devices: none -> 84.7 us  [local(): lax.all_gather(partial_out.astype(jnp.bfloat16), 'tensor')]
    psum x1 -> x0, waiting for transfers between devices: 68.4 us -> none  [local(): lax.psum(partial_out.astype(jnp.bfloat16), 'tensor').astype(jnp.float32)]
    reduce_sum x0 -> x1, other arithmetic: none -> 5.65 us  [local(): jnp.sum(lax.all_gather(partial_out.astype(jnp.bfloat16), 'tensor'), axis=0)]
    unnamed x18 -> x12, local copies, waits for them, and re-layouts: 5.19 us -> 0.76 us
    all_gather x1, blocking collectives: 27.3 us -> 25.4 us  [local(): lax.all_gather(w_out, ('section', 'dp'), axis=0, tiled=True)]
  transfers between devices with their start and end apart: 6 -> 6, of which waited for: 2 -> 2; matrix products, arithmetic and copies ran while one was open for 7% -> 4% of each run, Pallas kernels for 0% -> 0%
where the time goes in v1:
time: 182 us; the launch traced here: 181 us
  waiting for transfers between devices  100 us (55%)
  blocking collectives  25.4 us (14%)
  other arithmetic  15.9 us (9%)
  between operations  13.6 us (7%)
  local copies, waits for them, and re-layouts  10.2 us (6%)
  starting transfers between devices  8.43 us (5%)
  matrix products  7.76 us (4%)
    all_gather x1, waiting for transfers between devices, local(): lax.all_gather(partial_out.astype(jnp.bfloat16), 'tensor')  84.7 us
    all_gather x1, blocking collectives, local(): lax.all_gather(w_out, ('section', 'dp'), axis=0, tiled=True)  25.4 us
    all_gather x1, waiting for transfers between devices, local(): piece = lax.all_gather(w_qkv, ('section', 'dp'), axis=0, tiled=True)  14.7 us
    ppermute x2, starting transfers between devices, with_halo(): lax.ppermute(tail, axis, [(i, (i + 1) % count) for i in range(ends)])  5.82 us
    reduce_sum x1, other arithmetic, local(): jnp.sum(lax.all_gather(partial_out.astype(jnp.bfloat16), 'tensor'), axis=0)  5.65 us
    all_gather x1, local copies, waits for them, and re-layouts, local(): piece = lax.all_gather(w_qkv, ('section', 'dp'), axis=0, tiled=True)  5.3 us
    dot_general x1, matrix products, local(): jnp.dot(normed, piece.reshape(count, 3 * local_cols), preferred_element_t...  3.88 us
  transfers between devices with their start and end apart: 6, of which 2 were waited for; matrix products, arithmetic and copies ran while one was open for 4% of the time, Pallas kernels for 0%

profile of v1, /device:TPU:0, one launch (start us, length us, event | category | flops | bytes accessed | tf_op | source)
XLA Modules:
  0.0 181.3 jit_solution(3636883318832013305)
XLA Ops:
  6.5 0.0 all-gather.4.cloned.1.call-start
  6.5 0.7 all-gather.4.cloned.1.call-update
  7.3 0.0 all-gather.6.cloned.1.call-start
  7.3 0.7 fusion.32
  8.0 0.1 fusion.35
  8.1 1.3 collective-permute-start.3
  9.4 3.0 %collective-permute-start.2 = (s32[64]{0:T(128)S(1)}, s32[64]{0:T(128)S(1)}, u32[]{:S(2)}, u32[]{:S(2)}) collective-permute-start(s32[64]{0:T(128)S(1)} %get-tuple-element.14), channel_id=1, source_target_pairs={{0,4},{4,8},{8,12},{12,16},{16,20},{20,24},{24,28},{1,5},{5,9},{9,... | collective-permute-start | bytes 776 | tf_op jit(solution)/shard_map/ppermute | solution.py:18
  12.4 0.1 fusion.36
  12.5 2.0 %fusion.1 = f32[768]{0:T(1024)S(1)} fusion(bf16[768,1280]{1,0:T(8,128)(2,1)} %param.6), kind=kLoop, calls=%fused_computation.4 | loop fusion | flops 2948352 | bytes 1969152 | tf_op jit(solution)/shard_map/reduce_sum | solution.py:32
  14.5 25.4 %all_gather.13 = bf16[1280,320]{1,0:T(8,128)(2,1)} all-gather(bf16[160,320]{1,0:T(8,128)(2,1)} %param.11), channel_id=1, replica_groups=mesh['section'=4,'dp'=2,'tensor'=4] {'section','dp'}, dimensions={0}, use_global_device_ids=true | all-gather | bytes 921600 | tf_op jit(solution)/shard_map/all_gather | solution.py:66
  39.9 0.0 copy-done.2
  39.9 0.1 add.32
  39.9 0.0 collective-permute-done.3
  39.9 0.0 collective-permute-done.2
  39.9 0.1 pad_add_fusion.1
  40.0 0.1 slice.87
  40.1 0.0 copy-start
  40.1 0.0 copy-start.3
  40.2 14.7 %all-gather.4.cloned.1.call-done = bf16[1280,3,320]{2,0,1:T(8,128)(2,1)} async-done(((bf16[160,3,320]{2,0,1:T(8,128)(2,1)}), bf16[1280,3,320]{2,0,1:T(8,128)(2,1)}) %all-gather.4.cloned.1.call-update) | async-done | bytes 2457616 | tf_op jit(solution)/shard_map/all_gather | solution.py:34
  54.9 5.3 %copy.11 = bf16[1280,3,320]{0,2,1:T(8,128)(2,1)} copy(bf16[1280,3,320]{2,0,1:T(8,128)(2,1)} %all-gather.4.cloned.1.call-done) | data formatting | bytes 4915200 | tf_op jit(solution)/shard_map/all_gather | solution.py:34
  60.2 0.0 copy-done.3
  60.2 3.9 %add_convert_fusion = bf16[768,960]{0,1:T(8,128)(2,1)S(1)} fusion(bf16[1280,960]{0,1:T(8,128)(2,1)} %bitcast.53, bf16[768,1280]{1,0:T(8,128)(2,1)S(1)} %copy-done, f32[1280]{0:T(1024)S(1)} %copy-done.3, f32[768]{0:T(1024)S(1)} %add_rsqrt_fusion, f32[960]{0:T(1024)S(1)} %add.32), kind=kOutput, calls=%fused_computation.12 | convolution fusion | flops 1892843520 | bytes 5910272 | tf_op jit(solution)/shard_map/dot_general | solution.py:36
  64.1 0.8 fusion.34
  64.8 2.8 %collective-permute-start = (bf16[64,640]{0,1:T(8,128)(2,1)}, bf16[64,640]{0,1:T(8,128)(2,1)}, u32[]{:S(2)}, u32[]{:S(2)}) collective-permute-start(bf16[64,640]{0,1:T(8,128)(2,1)} %get-tuple-element.8), channel_id=1, source_target_pairs={{0,4},{4,8},{8,12},{12,16},{16,20},{20,24},{24,28},{1,5},{5,9},{9,... | collective-permute-start | bytes 245768 | tf_op jit(solution)/shard_map/ppermute | solution.py:18
  67.6 0.2 broadcast_compare_fusion
  67.8 0.8 slice.98
  68.6 0.1 slice.91
  68.7 1.3 collective-permute-start.1
  70.0 1.7 reshape.31
  71.6 0.0 collective-permute-done
  71.7 1.1 fusion.29
  72.7 0.2 fusion.27
  72.9 0.2 fusion.26
  73.1 0.2 fusion.25
  73.2 0.2 fusion.24
  73.4 0.0 collective-permute-done.1
  73.4 1.1 fusion.23
  74.6 0.1 fusion.33
  74.7 0.6 fusion.20
  75.3 1.8 fusion.37
  77.1 0.7 fusion.17
  77.9 0.3 copy.13
  78.2 0.1 copy-done.1
  78.3 2.5 %convolution_convert_fusion = bf16[768,1280]{1,0:T(8,128)(2,1)} fusion(bf16[1280,320]{1,0:T(8,128)(2,1)S(1)} %copy-done.1, bf16[40,8,6,128]{3,2,1,0:T(8,128)(2,1)S(1)} %bitcast.55), kind=kOutput, calls=%fused_computation.8 | convolution fusion | flops 630128640 | bytes 3276800 | tf_op jit(solution)/shard_map/dot_general | solution.py:64
  80.8 0.0 all-gather.6.cloned.1.call-update
  80.8 84.7 %all-gather.6.cloned.1.call-done = bf16[3072,1280]{1,0:T(8,128)(2,1)} async-done(((bf16[768,1280]{1,0:T(8,128)(2,1)}), bf16[3072,1280]{1,0:T(8,128)(2,1)}) %all-gather.6.cloned.1.call-update) | async-done | bytes 7864336 | tf_op jit(solution)/shard_map/all_gather | solution.py:70
  165.5 5.7 %reduce_sum.32 = bf16[768,1280]{1,0:T(8,128)(2,1)S(1)} reduce(bf16[4,768,1280]{2,1,0:T(8,128)(2,1)} %bitcast.51, bf16[]{:T(256)} %constant.16.clone.1), dimensions={0}, to_apply=%region_3.4 | reduce | flops 2949120 | bytes 9830402 | tf_op jit(solution)/shard_map/reduce_sum | solution.py:70
  171.1 3.3 %fusion.4 = bf16[768,1280]{1,0:T(8,128)(2,1)} fusion(bf16[768,1280]{1,0:T(8,128)(2,1)} %param.6, bf16[768,1280]{1,0:T(8,128)(2,1)S(1)} %reduce_sum.32), kind=kLoop, calls=%fused_computation.7 | loop fusion | flops 3932160 | bytes 5898240 | tf_op jit(solution)/shard_map/convert_element_type | solution.py:73
  (6 shorter events, 0.0 us)
Async XLA Ops:
  6.5 33.3 %copy-start.2 = (f32[3,320]{1,0:T(4,128)S(1)}, f32[3,320]{1,0:T(4,128)}, u32[]{:S(2)}) copy-start(f32[3,320]{1,0:T(4,128)} %param.10) | copy-start | bytes 11524
  6.5 48.3 %all-gather.4.cloned.1.call-start = ((), (), s32[]{:S(2)}) async-start(), calls=%async_computation | async-start | bytes 3317760 | tf_op jit(solution)/shard_map/all_gather | solution.py:34
  7.3 158.2 %all-gather.6.cloned.1.call-start = ((), (), s32[]{:S(2)}) async-start(), calls=%async_computation.1 | async-start | bytes 9830400 | tf_op jit(solution)/shard_map/all_gather | solution.py:70
  8.1 31.9 %collective-permute-start.3 = (s32[64]{0:T(128)S(1)}, s32[64]{0:T(128)S(1)}, u32[]{:S(2)}, u32[]{:S(2)}) collective-permute-start(s32[64]{0:T(128)S(1)} %get-tuple-element.13), channel_id=1, source_target_pairs={{4,0},{8,4},{12,8},{16,12},{20,16},{24,20},{28,24},{5,1},{9,5},{13... | collective-permute-start | bytes 776 | tf_op jit(solution)/shard_map/ppermute | solution.py:20
  9.4 30.6 %collective-permute-start.2 = (s32[64]{0:T(128)S(1)}, s32[64]{0:T(128)S(1)}, u32[]{:S(2)}, u32[]{:S(2)}) collective-permute-start(s32[64]{0:T(128)S(1)} %get-tuple-element.14), channel_id=1, source_target_pairs={{0,4},{4,8},{8,12},{12,16},{16,20},{20,24},{24,28},{1,5},{5,9},{9,... | collective-permute-start | bytes 776 | tf_op jit(solution)/shard_map/ppermute | solution.py:18
  40.1 20.0 %copy-start = (bf16[768,1280]{1,0:T(8,128)(2,1)S(1)}, bf16[768,1280]{1,0:T(8,128)(2,1)}, u32[]{:S(2)}) copy-start(bf16[768,1280]{1,0:T(8,128)(2,1)} %param.6) | copy-start | bytes 5898244
  40.1 20.0 %copy-start.3 = (f32[1280]{0:T(1024)S(1)}, f32[1280]{0:T(1024)}, u32[]{:S(2)}) copy-start(f32[1280]{0:T(1024)} %param.8) | copy-start | bytes 15364
  64.8 6.8 %collective-permute-start = (bf16[64,640]{0,1:T(8,128)(2,1)}, bf16[64,640]{0,1:T(8,128)(2,1)}, u32[]{:S(2)}, u32[]{:S(2)}) collective-permute-start(bf16[64,640]{0,1:T(8,128)(2,1)} %get-tuple-element.8), channel_id=1, source_target_pairs={{0,4},{4,8},{8,12},{12,16},{16,20},{20,24},{24,28},{1,5},{5,9},{9,... | collective-permute-start | bytes 245768 | tf_op jit(solution)/shard_map/ppermute | solution.py:18
  68.7 4.7 %collective-permute-start.1 = (bf16[64,640]{0,1:T(8,128)(2,1)S(1)}, bf16[64,640]{0,1:T(8,128)(2,1)}, u32[]{:S(2)}, u32[]{:S(2)}) collective-permute-start(bf16[64,640]{0,1:T(8,128)(2,1)S(1)} %get-tuple-element.7), channel_id=1, source_target_pairs={{4,0},{8,4},{12,8},{16,12},{20,16},{24,20},{28,24},{5,1},{9,5},{13... | collective-permute-start | bytes 245768 | tf_op jit(solution)/shard_map/ppermute | solution.py:20
  77.1 1.2 copy-start.1
Sparse Core Ops, SparseCore 0:
  9.0 45.8 all-gather.3
  81.0 84.4 all-gather.5
